TPU v7x, 32 devices: a whole 2x2x4 slice. The times are simulated.
32 devices in a mesh: wide: 4 (over y, core), narrow: 8 (over z, x).
Axes of the slice: x: 2, y: 2, z: 4, core: 2. Of those that a mesh axis runs over, the one named last changes fastest.
Arguments:
- queries: bfloat16 [8192, 128], P(('wide', 'narrow')), may hold values from -6 to 6
- index_rows: bfloat16 [262144, 128], P(('wide', 'narrow')), may hold values from -6 to 6
- lse_shift: float32 [8192], P('wide'), may hold values from 0 to 2.5
- loss_weight: float32 [8192], P('wide'), may hold values from 4 to 32
- positives: int32 [8192], P('wide'), may hold values from 0 to 16383
- tile_negs: int32 [64, 64], P('wide'), may hold values from 0 to 127
- fetch_owner: int32 [512, 1], P(('wide', 'narrow')), may hold values from 0 to 31; in each aligned block of 16 rows (0 to 15, 16 to 31, ...) at most 2 rows name the same one
- fetch_local: int32 [512], P(('wide', 'narrow')), may hold values from 0 to 63
Outputs:
- query_grad: float32 [8192, 128], P(('wide', 'narrow'))
- index_grad: float32 [262144, 128], P(('wide', 'narrow'))
Inputs may be any that keep to these rules, and one draw needn't show every extreme that they name: `fetch_owner`: among the 16 fetches of one device no owner is named more than 2 times, a bound that some block reaches.
All inputs are finite; a program needn't handle non-finite values.
Results may differ from a plain program's by a relative error of at most 0.0043.
Values may be sent and summed in bfloat16 or wider, within the bound.
A program may use at most 128 MiB of HBM per device.

v0:
```python
import math

import jax
import jax.numpy as jnp
from jax import lax
from jax.sharding import PartitionSpec as P

BLOCK = 128
QTILE = 128
CAP = 2


def slot_places(owners):
    fetch_count = owners.shape[0]
    position = jnp.arange(fetch_count, dtype=jnp.int32)
    same_owner = (owners[:, None] == owners[None, :]) & (position[None, :] < position[:, None])
    before = jnp.sum(same_owner.astype(jnp.int32), axis=1)
    return owners * CAP + before


def shards(
    queries, index_rows, lse_shift, loss_weight, positives, tile_negs, fetch_owner, fetch_local
):
    wide_count = lax.axis_size("wide")
    narrow_count = lax.axis_size("narrow")
    slots_all = wide_count * narrow_count * CAP
    feat_width = queries.shape[1]
    blocks_here = index_rows.shape[0] // BLOCK
    owners = fetch_owner[:, 0]
    fetch_count = owners.shape[0]
    places = slot_places(owners)
    grouped = lax.all_gather(queries, "narrow", axis=0, tiled=True)
    requests = jnp.full((slots_all,), -1, jnp.int32).at[places].set(fetch_local)
    asked_ids = lax.all_to_all(
        requests, ("wide", "narrow"), split_axis=0, concat_axis=0, tiled=True
    )
    stored = index_rows.reshape(blocks_here, BLOCK, feat_width)
    served = jnp.take(stored, jnp.maximum(asked_ids, 0), axis=0)
    arrived = lax.all_to_all(served, ("wide", "narrow"), split_axis=0, concat_axis=0, tiled=True)
    fetched = jnp.take(arrived, places, axis=0).reshape(fetch_count * BLOCK, feat_width)
    score_scale = 2.0 / math.sqrt(feat_width)
    narrow_pos = lax.axis_index("narrow")
    query_total = grouped.shape[0]
    block_size = min(512, query_total)
    block_count = query_total // block_size
    column_count = fetch_count * BLOCK
    lse_full = lse_shift + math.log(fetch_count * narrow_count * BLOCK)
    slot_ids = narrow_pos * fetch_count + jnp.arange(fetch_count, dtype=jnp.int32)
    tile_hit = jnp.any(tile_negs[:, :, None] == slot_ids[None, None, :], axis=1)
    query_hit = jnp.repeat(tile_hit, QTILE, axis=0)
    pos_hit = (positives // BLOCK)[:, None] == slot_ids[None, :]
    query_weight = jnp.logical_or(query_hit, pos_hit).astype(jnp.float32)
    column_ids = narrow_pos * column_count + jnp.arange(column_count, dtype=jnp.int32)

    def one_block(turn_idx, totals):
        block_grad, query_grad = totals
        row_start = turn_idx * block_size
        query_block = lax.dynamic_slice_in_dim(grouped, row_start, block_size, 0)
        row_weight = lax.dynamic_slice_in_dim(query_weight, row_start, block_size, 0)
        lse_rows = lax.dynamic_slice_in_dim(lse_full, row_start, block_size, 0)
        loss_rows = lax.dynamic_slice_in_dim(loss_weight, row_start, block_size, 0)
        pos_rows = lax.dynamic_slice_in_dim(positives, row_start, block_size, 0)
        scores = (
            lax.dot_general(
                query_block, fetched, (((1,), (1,)), ((), ())), preferred_element_type=jnp.float32
            )
            * score_scale
        )
        softmax_terms = jnp.exp(scores - lse_rows[:, None])
        weighted = (
            softmax_terms.reshape(block_size, fetch_count, BLOCK) * row_weight[:, :, None]
        ).reshape(block_size, column_count)
        target = (pos_rows[:, None] == column_ids[None, :]).astype(jnp.float32)
        logit_grad = (loss_rows[:, None] * (weighted - target)).astype(jnp.bfloat16)
        query_part = jnp.dot(logit_grad, fetched, preferred_element_type=jnp.float32) * score_scale
        query_grad = lax.dynamic_update_slice_in_dim(query_grad, query_part, row_start, 0)
        block_grad = block_grad + lax.dot_general(
            logit_grad, query_block, (((0,), (0,)), ((), ())), preferred_element_type=jnp.float32
        )
        return (block_grad, query_grad)

    zeros_init = (
        jnp.zeros((column_count, feat_width), jnp.float32),
        jnp.zeros((query_total, feat_width), jnp.float32),
    )
    block_grad, query_grad = lax.fori_loop(0, block_count, one_block, zeros_init)
    block_send = (
        (block_grad * score_scale).astype(jnp.bfloat16).reshape(fetch_count, BLOCK, feat_width)
    )
    outgoing = jnp.zeros((slots_all, BLOCK, feat_width), jnp.bfloat16).at[places].set(block_send)
    returned = lax.all_to_all(outgoing, ("wide", "narrow"), split_axis=0, concat_axis=0, tiled=True)
    onehot = (asked_ids[None, :] == jnp.arange(blocks_here, dtype=jnp.int32)[:, None]).astype(
        jnp.bfloat16
    )
    index_grad = jnp.dot(
        onehot, returned.reshape(slots_all, BLOCK * feat_width), preferred_element_type=jnp.float32
    )
    index_grad = index_grad.reshape(blocks_here * BLOCK, feat_width)
    query_out = lax.psum_scatter(query_grad, "narrow", scatter_dimension=0, tiled=True)
    return (query_out, index_grad)


def solution(mesh):
    in_specs = (
        P(("wide", "narrow"), None),
        P(("wide", "narrow"), None),
        P("wide"),
        P("wide"),
        P("wide"),
        P("wide", None),
        P(("wide", "narrow"), None),
        P(("wide", "narrow")),
    )
    out_specs = (P(("wide", "narrow"), None), P(("wide", "narrow"), None))
    return jax.shard_map(shards, mesh=mesh, in_specs=in_specs, out_specs=out_specs, check_vma=False)
```

profile of v0, /device:TPU:0, one launch (start us, length us, event | category | flops | bytes accessed | tf_op | source)
XLA Modules:
  0.0 256.1 jit_solution(4215112146317676985)
XLA Ops:
  9.7 14.2 %all_to_all.22 = s32[32,2,1]{1,2,0:T(1,128)S(1)} all-to-all(s32[32,2,1]{1,2,0:T(1,128)S(1)} %bitcast.53), channel_id=1, replica_groups=mesh['wide'=4,'narrow'=8] {'wide','narrow'}, dimensions={0} | all-to-all | bytes 512 | tf_op jit(solution)/shard_map/all_to_all | solution.py:34
  25.4 2.1 gather_fusion
  27.6 3.2 %broadcast_select_fusion = bf16[64,128,128]{2,1,0:T(8,128)(2,1)} fusion(bf16[64,128,128]{2,1,0:T(8,128)(2,1)} %gather_fusion, pred[64]{0:T(512)(128)(4,1)S(1)} %maximum_compare_fusion), kind=kLoop, calls=%fused_computation.21 | loop fusion | flops 1048576 | bytes 4194368 | tf_op jit(solution)/shard_map/jit(_take)/select_n | solution.py:38
  30.7 3.6 %all-to-all-start.1 = ((bf16[64,128,128]{2,1,0:T(8,128)(2,1)}), bf16[64,128,128]{2,1,0:T(8,128)(2,1)}, u32[]{:S(2)}, u32[]{:S(2)}) async-start(bf16[64,128,128]{2,1,0:T(8,128)(2,1)} %broadcast_select_fusion), calls=%async_computation.1 | async-start | bytes 4194304 | tf_op jit(solution)/shard_map/all_to_all | solution.py:39
  36.3 70.8 %all_gather.3 = bf16[2048,128]{1,0:T(8,128)(2,1)} all-gather(bf16[256,128]{1,0:T(8,128)(2,1)S(1)} %copy-done.4), channel_id=1, replica_groups=mesh['wide'=4,'narrow'=8] {'narrow'}, dimensions={0}, use_global_device_ids=true | all-gather | bytes 589824 | tf_op jit(solution)/shard_map/all_gather | solution.py:32
  107.1 3.0 %gather_fusion.1 = bf16[16,128,128]{2,1,0:T(8,128)(2,1)} fusion(bf16[64,128,128]{2,1,0:T(8,128)(2,1)} %all-to-all-done.1, s32[1024]{0:T(1024)S(1)} %pad_clamp_fusion), kind=kCustom, calls=%fused_computation.1 | custom fusion | bytes 1048640 | tf_op jit(solution)/shard_map/jit(_take)/gather | solution.py:40
  110.1 2.2 bitcast_select_fusion
  113.3 47.1 %while.16 = (s32[]{:T(128)}, f32[2048,128]{1,0:T(8,128)S(1)}, f32[2048,128]{1,0:T(8,128)}, f32[2048]{0:T(1024)}, bf16[2048,128]{1,0:T(8,128)(2,1)}, /*index=5*/b...) while((s32[]{:T(128)}, f32[2048,128]{1,0:T(8,128)S(1)}, ...), condition=%wide.region_4.5_spmd.clone, body=%wide.region_3.4_spmd.clone.sunk | while | flops 814286848 | bytes 28969236 | solution.py:86
  116.3 3.3 %fusion.39 = bf16[512,2048]{1,0:T(8,128)(2,1)S(1)} fusion(f32[64,8,16,128]{3,2,1,0:T(8,128)S(1)} %bitcast.51, bf16[2048,128]{1,0:T(8,128)(2,1)S(1)} %copy-done.2, s32[2048]{0:T(1024)S(1)} %iota_add_fusion.3, f32[512]{0:T(512)S(1)} %dynamic_slice.54, f32[512]{0:T(512)S(1)} %dynamic_slice.55, s32[512]{0:T(512)S(1)} %dynamic_slice.56, ...), kind=kOutput, calls=%fused_computation.8.clone.1 | convolution fusion | flops 276824064 | bytes 6961156 | tf_op jit(solution)/shard_map/while/body/eval_jaxpr/dot_general | solution.py:64
  122.4 2.6 %convolution_add_fusion.2 = f32[2048,128]{1,0:T(8,128)S(1)} fusion(bf16[512,2048]{1,0:T(8,128)(2,1)} %copy-done.1, f32[2048,128]{1,0:T(8,128)S(1)} %get-tuple-element.310, pred[]{:T(512)S(6)} %compare.5, bf16[2048,128]{1,0:T(8,128)(2,1)} %get-tuple-element.327, s32[]{:T(128)S(6)} %select_n.49), kind=kOutput, calls=%fused_computation.9.clone.1 | convolution fusion | flops 268959744 | bytes 4325381 | tf_op jit(solution)/shard_map/while/body/eval_jaxpr/dot_general | solution.py:77
  128.1 3.3 %fusion.39 = bf16[512,2048]{1,0:T(8,128)(2,1)S(1)} fusion(f32[64,8,16,128]{3,2,1,0:T(8,128)S(1)} %bitcast.51, bf16[2048,128]{1,0:T(8,128)(2,1)S(1)} %copy-done.2, s32[2048]{0:T(1024)S(1)} %iota_add_fusion.3, f32[512]{0:T(512)S(1)} %dynamic_slice.54, f32[512]{0:T(512)S(1)} %dynamic_slice.55, s32[512]{0:T(512)S(1)} %dynamic_slice.56, ...), kind=kOutput, calls=%fused_computation.8.clone.1 | convolution fusion | flops 276824064 | bytes 6961156 | tf_op jit(solution)/shard_map/while/body/eval_jaxpr/dot_general | solution.py:64
  134.2 2.6 %convolution_add_fusion.2 = f32[2048,128]{1,0:T(8,128)S(1)} fusion(bf16[512,2048]{1,0:T(8,128)(2,1)} %copy-done.1, f32[2048,128]{1,0:T(8,128)S(1)} %get-tuple-element.310, pred[]{:T(512)S(6)} %compare.5, bf16[2048,128]{1,0:T(8,128)(2,1)} %get-tuple-element.327, s32[]{:T(128)S(6)} %select_n.49), kind=kOutput, calls=%fused_computation.9.clone.1 | convolution fusion | flops 268959744 | bytes 4325381 | tf_op jit(solution)/shard_map/while/body/eval_jaxpr/dot_general | solution.py:77
  139.9 3.3 %fusion.39 = bf16[512,2048]{1,0:T(8,128)(2,1)S(1)} fusion(f32[64,8,16,128]{3,2,1,0:T(8,128)S(1)} %bitcast.51, bf16[2048,128]{1,0:T(8,128)(2,1)S(1)} %copy-done.2, s32[2048]{0:T(1024)S(1)} %iota_add_fusion.3, f32[512]{0:T(512)S(1)} %dynamic_slice.54, f32[512]{0:T(512)S(1)} %dynamic_slice.55, s32[512]{0:T(512)S(1)} %dynamic_slice.56, ...), kind=kOutput, calls=%fused_computation.8.clone.1 | convolution fusion | flops 276824064 | bytes 6961156 | tf_op jit(solution)/shard_map/while/body/eval_jaxpr/dot_general | solution.py:64
  144.5 1.4 fusion.40
  145.9 2.6 %convolution_add_fusion.2 = f32[2048,128]{1,0:T(8,128)S(1)} fusion(bf16[512,2048]{1,0:T(8,128)(2,1)} %copy-done.1, f32[2048,128]{1,0:T(8,128)S(1)} %get-tuple-element.310, pred[]{:T(512)S(6)} %compare.5, bf16[2048,128]{1,0:T(8,128)(2,1)} %get-tuple-element.327, s32[]{:T(128)S(6)} %select_n.49), kind=kOutput, calls=%fused_computation.9.clone.1 | convolution fusion | flops 268959744 | bytes 4325381 | tf_op jit(solution)/shard_map/while/body/eval_jaxpr/dot_general | solution.py:77
  151.6 3.3 %fusion.39 = bf16[512,2048]{1,0:T(8,128)(2,1)S(1)} fusion(f32[64,8,16,128]{3,2,1,0:T(8,128)S(1)} %bitcast.51, bf16[2048,128]{1,0:T(8,128)(2,1)S(1)} %copy-done.2, s32[2048]{0:T(1024)S(1)} %iota_add_fusion.3, f32[512]{0:T(512)S(1)} %dynamic_slice.54, f32[512]{0:T(512)S(1)} %dynamic_slice.55, s32[512]{0:T(512)S(1)} %dynamic_slice.56, ...), kind=kOutput, calls=%fused_computation.8.clone.1 | convolution fusion | flops 276824064 | bytes 6961156 | tf_op jit(solution)/shard_map/while/body/eval_jaxpr/dot_general | solution.py:64
  157.7 2.6 %convolution_add_fusion.2 = f32[2048,128]{1,0:T(8,128)S(1)} fusion(bf16[512,2048]{1,0:T(8,128)(2,1)} %copy-done.1, f32[2048,128]{1,0:T(8,128)S(1)} %get-tuple-element.310, pred[]{:T(512)S(6)} %compare.5, bf16[2048,128]{1,0:T(8,128)(2,1)} %get-tuple-element.327, s32[]{:T(128)S(6)} %select_n.49), kind=kOutput, calls=%fused_computation.9.clone.1 | convolution fusion | flops 268959744 | bytes 4325381 | tf_op jit(solution)/shard_map/while/body/eval_jaxpr/dot_general | solution.py:77
  161.2 1.8 broadcast_in_dim.66
  163.1 2.6 %scatter_fusion = bf16[64,128,128]{2,1,0:T(8,128)(2,1)} fusion(bf16[64,128,128]{2,1,0:T(8,128)(2,1)} %broadcast_in_dim.66, s32[16]{0:T(128)S(1)} %bitcast.56, bf16[16,128,128]{2,1,0:T(8,128)(2,1)S(1)} %bitcast.52), kind=kCustom, calls=%fused_computation.3 | custom fusion | bytes 1572928 | tf_op jit(solution)/shard_map/scatter | solution.py:90
  165.6 3.5 %all-to-all-start.2 = ((bf16[64,128,128]{2,1,0:T(8,128)(2,1)}), bf16[64,128,128]{2,1,0:T(8,128)(2,1)}, u32[]{:S(2)}, u32[]{:S(2)}) async-start(bf16[64,128,128]{2,1,0:T(8,128)(2,1)} %scatter_fusion), calls=%async_computation.3 | async-start | bytes 4194304 | tf_op jit(solution)/shard_map/all_to_all | solution.py:91
  169.9 57.8 %all-to-all-done.2 = bf16[64,128,128]{2,1,0:T(8,128)(2,1)} async-done(((bf16[64,128,128]{2,1,0:T(8,128)(2,1)}), bf16[64,128,128]{2,1,0:T(8,128)(2,1)}, u32[]{:S(2)}, u32[]{:S(2)}) %all-to-all-start.2) | async-done | bytes 2097184 | tf_op jit(solution)/shard_map/all_to_all | solution.py:91
  227.7 5.2 %fusion.10 = f32[64,16384]{1,0:T(8,128)} fusion(bf16[8,8,128,128]{3,2,1,0:T(8,128)(2,1)} %bitcast.12, s32[64]{0:T(128)S(1)} %all_to_all.16), kind=kOutput, calls=%fused_computation.18 | convolution fusion | flops 134221824 | bytes 6291712 | tf_op jit(solution)/shard_map/dot_general | solution.py:95
  232.9 4.9 %reshape.79 = f32[8192,128]{1,0:T(8,128)} reshape(f32[64,16384]{1,0:T(8,128)} %fusion.10) | data formatting | bytes 8388608 | tf_op jit(solution)/shard_map/reshape | solution.py:98
  237.8 11.4 %reduce-scatter.2.cloned.1.call-done = f32[256,128]{1,0:T(8,128)} async-done(((f32[2048,128]{1,0:T(8,128)}), f32[256,128]{1,0:T(8,128)}) %reduce-scatter.2.cloned.1.call-update) | async-done | bytes 131088 | tf_op jit(solution)/shard_map/reduce_scatter | solution.py:99
  (78 shorter events, 30.1 us)
Async XLA Ops:
  7.2 18.3 %copy-start = (bf16[8192,128]{1,0:T(8,128)(2,1)S(1)}, bf16[8192,128]{1,0:T(8,128)(2,1)}, u32[]{:S(2)}) copy-start(bf16[8192,128]{1,0:T(8,128)(2,1)} %param.11) | copy-start | bytes 6291460
  30.7 3.7 %copy-start.6 = (s32[16,64]{1,0:T(8,128)S(1)}, s32[16,64]{1,0:T(8,128)}, u32[]{:S(2)}) copy-start(s32[16,64]{1,0:T(8,128)} %param.15) | copy-start | bytes 12292
  30.7 4.1 %copy-start.5 = (s32[2048]{0:T(1024)S(1)}, s32[2048]{0:T(1024)}, u32[]{:S(2)}) copy-start(s32[2048]{0:T(1024)} %param.14) | copy-start | bytes 24580
  30.7 5.5 %copy-start.7 = (f32[2048]{0:T(1024)S(1)}, f32[2048]{0:T(1024)}, u32[]{:S(2)}) copy-start(f32[2048]{0:T(1024)} %param.12) | copy-start | bytes 24580
  30.7 5.5 %copy-start.4 = (bf16[256,128]{1,0:T(8,128)(2,1)S(1)}, bf16[256,128]{1,0:T(8,128)(2,1)}, u32[]{:S(2)}) copy-start(bf16[256,128]{1,0:T(8,128)(2,1)} %param.10) | copy-start | bytes 196612
  30.7 76.3 %all-to-all-start.1 = ((bf16[64,128,128]{2,1,0:T(8,128)(2,1)}), bf16[64,128,128]{2,1,0:T(8,128)(2,1)}, u32[]{:S(2)}, u32[]{:S(2)}) async-start(bf16[64,128,128]{2,1,0:T(8,128)(2,1)} %broadcast_select_fusion), calls=%async_computation.1 | async-start | bytes 4194304 | tf_op jit(solution)/shard_map/all_to_all | solution.py:39
  114.3 2.1 copy-start.2
  119.7 1.3 copy-start.1
  126.0 2.1 copy-start.2
  131.4 1.3 copy-start.1
  137.8 2.1 copy-start.2
  143.2 1.3 copy-start.1
  149.6 2.1 copy-start.2
  155.0 1.3 copy-start.1
  161.2 1.8 copy-start.3
  165.6 62.1 %all-to-all-start.2 = ((bf16[64,128,128]{2,1,0:T(8,128)(2,1)}), bf16[64,128,128]{2,1,0:T(8,128)(2,1)}, u32[]{:S(2)}, u32[]{:S(2)}) async-start(bf16[64,128,128]{2,1,0:T(8,128)(2,1)} %scatter_fusion), calls=%async_computation.3 | async-start | bytes 4194304 | tf_op jit(solution)/shard_map/all_to_all | solution.py:91
  169.1 80.1 %reduce-scatter.2.cloned.1.call-start = ((), (), s32[]{:S(2)}) async-start(), calls=%async_computation.4 | async-start | bytes 1179648 | tf_op jit(solution)/shard_map/reduce_scatter | solution.py:99
Sparse Core Ops, SparseCore 0:
  173.9 75.2 reduce-scatter.1
where the time goes:
time: 257 us; the launch traced here: 256 us
  blocking collectives  85 us (33%)
  waiting for transfers between devices  69.9 us (27%)
  matrix products  34.7 us (14%)
  local copies, waits for them, and re-layouts  34.5 us (13%)
  between operations  14.2 us (6%)
  other arithmetic  10.4 us (4%)
  starting transfers between devices  7.16 us (3%)
    all_gather x1, blocking collectives, shards(): grouped = lax.all_gather(queries, 'narrow', axis=0, tiled=True)  70.8 us
    all_to_all x1, waiting for transfers between devices, shards(): lax.all_to_all(outgoing, ('wide', 'narrow'), split_axis=0, concat_axis=0,...  57.8 us
    all_to_all x1, blocking collectives, shards(): lax.all_to_all(requests, ('wide', 'narrow'), split_axis=0, concat_axis=0,...  14.2 us
    dot_general x4, matrix products, one_block(): lax.dot_general(query_block, fetched, (((1,), (1,)), ((), ())), preferred...  13.2 us
    reduce_scatter x1, waiting for transfers between devices, shards(): lax.psum_scatter(query_grad, 'narrow', scatter_dimension=0, tiled=True)  11.4 us
    dot_general x4, matrix products, one_block(): lax.dot_general(logit_grad, query_block, (((0,), (0,)), ((), ())), prefer...  10.5 us
    dot_general x4, matrix products, one_block(): jnp.dot(logit_grad, fetched, preferred_element_type=jnp.float32)  5.68 us
    while x16, local copies, waits for them, and re-layouts  5.27 us
  transfers between devices with their start and end apart: 3, of which 2 were waited for; matrix products, arithmetic and copies ran while one was open for 5% of the time, Pallas kernels for 0%

commit v1 on v0

v1 whole, which is shorter than its diff:
```python
import functools
import math

import jax
import jax.numpy as jnp
from jax import lax
from jax.experimental import pallas as pl
from jax.experimental.pallas import tpu as pltpu
from jax.sharding import PartitionSpec as P

BLOCK = 128
QTILE = 128
CAP = 2
LANES = 128
CORES = 2
MESH = pl.DeviceIdType.MESH
VMEM_LIMIT = 56 * 1024 * 1024
FAR_BELOW = -1e30


def place_counts(wide_count, narrow_count):
    x_count = 1 << (int(math.log2(narrow_count)) // 2)
    return wide_count // CORES, narrow_count // x_count, x_count


def coordinates(x_count):
    wide, narrow = lax.axis_index("wide"), lax.axis_index("narrow")
    return wide // CORES, wide % CORES, narrow // x_count, narrow % x_count


def greet(peers):
    barrier = pltpu.get_barrier_semaphore()
    for peer in peers:
        pl.semaphore_signal(barrier, inc=1, device_id=peer, device_id_type=MESH)
    pl.semaphore_wait(barrier, len(peers))


def gather_kernel(
    y_count, z_count, x_count, query_ref, aux_ref, query_all, aux_all, own_sem, *sems
):
    y, core, z, x = coordinates(x_count)
    narrow_count = z_count * x_count

    def device(dy, other, dz, dx):
        wide = lax.rem(y + dy, y_count) * CORES + (1 - core if other else core)
        return wide, lax.rem(z + dz, z_count) * x_count + lax.rem(x + dx, x_count)

    def number(place):
        return place[0] * narrow_count + place[1]

    plane = [(dy, dx) for dy in range(y_count) for dx in range(x_count)][1:]
    z_peers = [device(0, False, dz, 0) for dz in range(1, z_count)]
    plane_peers = [device(dy, False, 0, dx) for dy, dx in plane]
    buddy = device(0, True, 0, 0)
    greet(z_peers + plane_peers + [buddy])
    me = number(device(0, False, 0, 0))
    pairs = (
        (query_ref, query_all, sems[0], sems[1]),
        (aux_ref, aux_all, sems[2], sems[3]),
    )
    sent = []

    def send(chunk, peer, own):
        for source, whole, send_sem, recv_sem in pairs:
            copy = pltpu.make_async_remote_copy(
                src_ref=source if own else whole.at[chunk],
                dst_ref=whole.at[chunk],
                send_sem=send_sem.at[len(sent) // 2],
                recv_sem=recv_sem.at[chunk],
                device_id=peer,
                device_id_type=MESH,
            )
            copy.start()
            sent.append(copy)

    def arrive(chunk):
        for source, whole, send_sem, recv_sem in pairs:
            pltpu.make_async_remote_copy(
                src_ref=source,
                dst_ref=whole.at[chunk],
                send_sem=send_sem.at[0],
                recv_sem=recv_sem.at[chunk],
                device_id=buddy,
                device_id_type=MESH,
            ).wait_recv()

    local = [
        pltpu.make_async_copy(source, whole.at[me], own_sem.at[i])
        for i, (source, whole, _, _) in enumerate(pairs)
    ]
    for copy in local:
        copy.start()
    for peer in z_peers + plane_peers + [buddy]:
        send(me, peer, True)
    for dz in range(1, z_count):
        chunk = number(device(0, False, dz, 0))
        arrive(chunk)
        for peer in plane_peers + [buddy]:
            send(chunk, peer, False)
    for dz in range(z_count):
        for dy, dx in plane:
            chunk = number(device(dy, False, dz, dx))
            arrive(chunk)
            send(chunk, buddy, False)
    for dz in range(z_count):
        for dy, dx in [(0, 0)] + plane:
            arrive(number(device(dy, True, dz, dx)))
    for copy in sent:
        copy.wait_send()
    for copy in local:
        copy.wait()


def gather_all(queries, aux, counts):
    y_count, z_count, x_count = counts
    devices = y_count * CORES * z_count * x_count
    in_plane = y_count * x_count
    sends = (z_count - 1) + (in_plane - 1) * z_count + in_plane * z_count
    return pl.pallas_call(
        functools.partial(gather_kernel, *counts),
        out_shape=(
            jax.ShapeDtypeStruct((devices, *queries.shape), queries.dtype),
            jax.ShapeDtypeStruct((devices, *aux.shape), aux.dtype),
        ),
        in_specs=[pl.BlockSpec(memory_space=pltpu.VMEM)] * 2,
        out_specs=[pl.BlockSpec(memory_space=pltpu.VMEM)] * 2,
        scratch_shapes=[
            pltpu.SemaphoreType.DMA((2,)),
            pltpu.SemaphoreType.DMA((sends,)),
            pltpu.SemaphoreType.DMA((devices,)),
            pltpu.SemaphoreType.DMA((sends,)),
            pltpu.SemaphoreType.DMA((devices,)),
        ],
        compiler_params=pltpu.CompilerParams(
            collective_id=0, has_side_effects=True, vmem_limit_bytes=VMEM_LIMIT
        ),
    )(queries, aux)


def work_kernel(
    score_scale,
    me_ref,
    owner_ref,
    local_ref,
    index_ref,
    query_ref,
    bias_ref,
    loss_ref,
    pos_ref,
    negs_ref,
    dq_ref,
    index_grad_ref,
    names,
    bias_now,
    rel_now,
    block_sum,
):
    fetch_total = owner_ref.shape[0]
    tile_total = bias_ref.shape[0]
    groups = lax.axis_size("wide")
    group_tiles = tile_total // groups
    group_slots = fetch_total // groups
    chunk_tiles = min(4, group_tiles)
    chunk = chunk_tiles * QTILE
    me = me_ref[0]
    log2_scale = score_scale * math.log2(math.e)

    def list_one(i, count):
        names[count] = i
        return count + (owner_ref[i] == me).astype(jnp.int32)

    count = lax.fori_loop(0, fetch_total, list_one, jnp.int32(0), unroll=8)
    dq_ref[...] = jnp.zeros_like(dq_ref)
    index_grad_ref[...] = jnp.zeros_like(index_grad_ref)
    row_ids = lax.broadcasted_iota(jnp.int32, (BLOCK, QTILE), 0)

    @pl.loop(0, count)
    def _(i):
        fetch = names[i]
        group = fetch // group_slots
        slot = fetch % group_slots
        rows = pl.ds(pl.multiple_of(local_ref[fetch] * BLOCK, BLOCK), BLOCK)
        block = index_ref[rows, :]
        block_t = block.astype(jnp.float32).T.astype(jnp.bfloat16)
        tiles = pl.ds(pl.multiple_of(group * group_tiles, 8), group_tiles)
        hit = jnp.any(negs_ref[tiles, :] == slot, axis=1, keepdims=True)
        rel = pos_ref[tiles, :] - slot * BLOCK
        inside = jnp.logical_and(rel >= 0, rel < BLOCK)
        bias_now[...] = jnp.where(jnp.logical_or(hit, inside), bias_ref[tiles, :], FAR_BELOW)
        rel_now[...] = rel
        block_sum[...] = jnp.zeros_like(block_sum)
        for turn in range(group_tiles // chunk_tiles):
            first = group * group_tiles + turn * chunk_tiles
            query = query_ref[pl.ds(pl.multiple_of(first * QTILE, chunk), chunk), :]
            scores = lax.dot_general(
                block, query, (((1,), (1,)), ((), ())), preferred_element_type=jnp.float32
            )
            parts = []
            for t in range(chunk_tiles):
                at = turn * chunk_tiles + t
                grown = jnp.exp2(
                    scores[:, t * QTILE : (t + 1) * QTILE] * log2_scale + bias_now[at : at + 1, :]
                )
                less = grown - loss_ref[pl.ds(first + t, 1), :]
                grad = jnp.where(row_ids == rel_now[at : at + 1, :], less, grown)
                parts.append(grad.astype(jnp.bfloat16))
            logit_grad = jnp.concatenate(parts, axis=1)
            block_sum[...] += jnp.dot(logit_grad, query, preferred_element_type=jnp.float32)
            part = jnp.dot(block_t, logit_grad, preferred_element_type=jnp.float32)
            for t in range(chunk_tiles):
                dq_ref[first + t] += part[:, t * QTILE : (t + 1) * QTILE]
        term = (block_sum[...] * score_scale).astype(jnp.bfloat16).astype(jnp.float32)
        index_grad_ref[rows, :] += term


def work(me, owner, local, index_rows, query_all, bias, loss, pos, negs, score_scale):
    feat_width = index_rows.shape[1]
    tile_total = bias.shape[0]
    group_tiles = tile_total // lax.axis_size("wide")
    smem, vmem = (pl.BlockSpec(memory_space=m) for m in (pltpu.SMEM, pltpu.VMEM))
    return pl.pallas_call(
        functools.partial(work_kernel, score_scale),
        out_shape=(
            jax.ShapeDtypeStruct((tile_total, feat_width, QTILE), jnp.float32),
            jax.ShapeDtypeStruct(index_rows.shape, jnp.float32),
        ),
        in_specs=[smem] * 3 + [vmem] * 6,
        out_specs=[vmem] * 2,
        scratch_shapes=[
            pltpu.SMEM((owner.shape[0] + 1,), jnp.int32),
            pltpu.VMEM((group_tiles, QTILE), jnp.float32),
            pltpu.VMEM((group_tiles, QTILE), jnp.int32),
            pltpu.VMEM((BLOCK, feat_width), jnp.float32),
        ],
        compiler_params=pltpu.CompilerParams(vmem_limit_bytes=VMEM_LIMIT),
    )(me, owner, local, index_rows, query_all, bias, loss, pos, negs)


def scatter_kernel(
    y_count,
    z_count,
    x_count,
    score_scale,
    part_ref,
    out_ref,
    from_buddy,
    plane_send,
    plane_recv,
    column_send,
    column_recv,
    *sems,
):
    y, core, z, x = coordinates(x_count)
    narrow_count = z_count * x_count
    a_send, a_recv, b_send, b_recv, c_send, c_recv = sems

    def device(dy, other, dz, dx):
        wide = lax.rem(y + dy, y_count) * CORES + (1 - core if other else core)
        return wide, lax.rem(z + dz, z_count) * x_count + lax.rem(x + dx, x_count)

    def number(place):
        return place[0] * narrow_count + place[1]

    def remote(source, target, send_sem, recv_sem, peer):
        return pltpu.make_async_remote_copy(
            src_ref=source,
            dst_ref=target,
            send_sem=send_sem,
            recv_sem=recv_sem,
            device_id=peer,
            device_id_type=MESH,
        )

    shifts = [(dy, dx) for dy in range(y_count) for dx in range(x_count)]
    plane = shifts[1:]
    buddy = device(0, True, 0, 0)
    z_peers = [device(0, False, dz, 0) for dz in range(1, z_count)]
    plane_peers = [device(dy, False, 0, dx) for dy, dx in plane]
    greet(z_peers + plane_peers + [buddy])
    order = [
        (p, dz) for dz in list(range(1, z_count)) + [0] for p in range(1, len(shifts))
    ] + [(0, dz) for dz in list(range(1, z_count)) + [0]]
    to_buddy = {}
    for p, dz in order:
        at = p * z_count + dz
        dy, dx = shifts[p]
        to_buddy[p, dz] = remote(
            part_ref.at[number(device(dy, True, dz, dx))],
            from_buddy.at[at],
            a_send.at[at],
            a_recv.at[at],
            buddy,
        )
        to_buddy[p, dz].start()
    in_plane, held = {}, {}
    for p, dz in order:
        at = p * z_count + dz
        dy, dx = shifts[p]
        to_buddy[p, dz].wait_recv()
        mine = part_ref.at[number(device(dy, False, dz, dx))]
        if p:
            slot = at - z_count
            plane_send[slot] = (mine[...] + from_buddy[at]).astype(jnp.bfloat16)
            in_plane[p, dz] = remote(
                plane_send.at[slot],
                plane_recv.at[slot],
                b_send.at[slot],
                b_recv.at[slot],
                plane_peers[p - 1],
            )
            in_plane[p, dz].start()
    columns = {}
    for dz in list(range(1, z_count)) + [0]:
        total = part_ref.at[number(device(0, False, dz, 0))][...] + from_buddy[dz]
        for p in range(1, len(shifts)):
            in_plane[p, dz].wait_recv()
            total += plane_recv[(p - 1) * z_count + dz].astype(jnp.float32)
        if dz:
            column_send[dz - 1] = total.astype(jnp.bfloat16)
            columns[dz] = remote(
                column_send.at[dz - 1],
                column_recv.at[dz - 1],
                c_send.at[dz - 1],
                c_recv.at[dz - 1],
                z_peers[dz - 1],
            )
            columns[dz].start()
    for dz in range(1, z_count):
        columns[dz].wait_recv()
        total += column_recv[dz - 1].astype(jnp.float32)
    for t in range(total.shape[0]):
        out_ref[t * QTILE : (t + 1) * QTILE, :] = total[t].T * score_scale
    for copy in [*to_buddy.values(), *in_plane.values(), *columns.values()]:
        copy.wait_send()


def scatter_all(partial, counts, score_scale):
    y_count, z_count, x_count = counts
    devices, tiles, feat_width, width = partial.shape
    half = devices // CORES
    passed = half - z_count
    block = (tiles, feat_width, width)
    return pl.pallas_call(
        functools.partial(scatter_kernel, *counts, score_scale),
        out_shape=jax.ShapeDtypeStruct((tiles * width, feat_width), jnp.float32),
        in_specs=[pl.BlockSpec(memory_space=pltpu.VMEM)],
        out_specs=pl.BlockSpec(memory_space=pltpu.VMEM),
        scratch_shapes=[
            pltpu.VMEM((half, *block), jnp.float32),
            pltpu.VMEM((passed, *block), jnp.bfloat16),
            pltpu.VMEM((passed, *block), jnp.bfloat16),
            pltpu.VMEM((z_count - 1, *block), jnp.bfloat16),
            pltpu.VMEM((z_count - 1, *block), jnp.bfloat16),
            pltpu.SemaphoreType.DMA((half,)),
            pltpu.SemaphoreType.DMA((half,)),
            pltpu.SemaphoreType.DMA((passed,)),
            pltpu.SemaphoreType.DMA((passed,)),
            pltpu.SemaphoreType.DMA((z_count - 1,)),
            pltpu.SemaphoreType.DMA((z_count - 1,)),
        ],
        compiler_params=pltpu.CompilerParams(
            collective_id=1, has_side_effects=True, vmem_limit_bytes=VMEM_LIMIT
        ),
    )(partial)


def shards(
    queries, index_rows, lse_shift, loss_weight, positives, tile_negs, fetch_owner, fetch_local
):
    wide_count = lax.axis_size("wide")
    narrow_count = lax.axis_size("narrow")
    devices = wide_count * narrow_count
    counts = place_counts(wide_count, narrow_count)
    narrow_pos = lax.axis_index("narrow")
    feat_width = queries.shape[1]
    own_queries = queries.shape[0]
    fetch_count = fetch_local.shape[0]
    negs_width = tile_negs.shape[1]
    score_scale = 2.0 / math.sqrt(feat_width)

    def share(array):
        length = array.shape[0] // narrow_count
        return lax.dynamic_slice_in_dim(array, narrow_pos * length, length, 0)

    pieces = [
        share(lse_shift),
        share(loss_weight),
        share(positives).astype(jnp.float32),
        share(tile_negs.reshape(-1)).astype(jnp.float32),
        fetch_owner[:, 0].astype(jnp.float32),
        fetch_local.astype(jnp.float32),
    ]
    lengths = [p.shape[0] for p in pieces]
    used = sum(lengths)
    padded = -(-used // (8 * LANES)) * 8 * LANES
    aux = jnp.pad(jnp.concatenate(pieces), (0, padded - used)).reshape(-1, LANES)
    query_all, aux_all = gather_all(queries, aux, counts)
    aux_all = aux_all.reshape(devices, padded)
    unpacked, start = [], 0
    for length in lengths:
        unpacked.append(aux_all[:, start : start + length].reshape(-1))
        start += length
    lse, loss, pos, negs, owner, local = unpacked
    lse_full = lse + math.log(fetch_count * narrow_count * BLOCK)
    bias = ((jnp.log(loss) - lse_full) * math.log2(math.e)).reshape(-1, QTILE)
    me = (lax.axis_index("wide") * narrow_count + narrow_pos).reshape(1)
    partial, index_grad = work(
        me,
        owner.astype(jnp.int32),
        local.astype(jnp.int32),
        index_rows,
        query_all.reshape(-1, feat_width),
        bias,
        loss.reshape(-1, QTILE),
        pos.astype(jnp.int32).reshape(-1, QTILE),
        negs.astype(jnp.int32).reshape(-1, negs_width),
        score_scale,
    )
    tiles = own_queries // QTILE
    query_grad = scatter_all(
        partial.reshape(devices, tiles, feat_width, QTILE), counts, score_scale
    )
    return query_grad, index_grad


def solution(mesh):
    in_specs = (
        P(("wide", "narrow"), None),
        P(("wide", "narrow"), None),
        P("wide"),
        P("wide"),
        P("wide"),
        P("wide", None),
        P(("wide", "narrow"), None),
        P(("wide", "narrow")),
    )
    out_specs = (P(("wide", "narrow"), None), P(("wide", "narrow"), None))
    return jax.shard_map(shards, mesh=mesh, in_specs=in_specs, out_specs=out_specs, check_vma=False)
```

time: 257 us -> 138 us (0.54)
  Pallas kernels: 0 us -> 127 us
  blocking collectives: 85 us -> 0 us
  waiting for transfers between devices: 69.9 us -> 0 us
  matrix products: 34.7 us -> 0 us
  local copies, waits for them, and re-layouts: 34.5 us -> 8.1 us
  between operations: 14.2 us -> 0.68 us
  other arithmetic: 10.4 us -> 2.87 us
  starting transfers between devices: 7.16 us -> 0 us
    pallas_call x0 -> x3, Pallas kernels: none -> 127 us  [the longest x1 79.2 us: scatter_all(): pl.pallas_call(functools.partial(scatter_kernel, *counts, score_scale), o...]
    all_gather x1 -> x0, blocking collectives: 70.8 us -> none  [shards(): grouped = lax.all_gather(queries, 'narrow', axis=0, tiled=True)]
    all_to_all x2 -> x0, waiting for transfers between devices: 57.8 us -> none  [the longest x1 57.8 us: shards(): lax.all_to_all(outgoing, ('wide', 'narrow'), split_axis=0, concat_axis=0,...]
    dot_general x13 -> x0, matrix products: 34.7 us -> none  [the longest x4 13.2 us: one_block(): lax.dot_general(query_block, fetched, (((1,), (1,)), ((), ())), preferred...]
    all_to_all x1 -> x0, blocking collectives: 14.2 us -> none  [shards(): lax.all_to_all(requests, ('wide', 'narrow'), split_axis=0, concat_axis=0,...]
    reduce_scatter x1 -> x0, waiting for transfers between devices: 11.4 us -> none  [shards(): lax.psum_scatter(query_grad, 'narrow', scatter_dimension=0, tiled=True)]
    all_to_all x2 -> x0, starting transfers between devices: 7.12 us -> none  [the longest x1 3.63 us: shards(): lax.all_to_all(served, ('wide', 'narrow'), split_axis=0, concat_axis=0, t...]
    dynamic_slice x16 -> x2, local copies, waits for them, and re-layouts: 7.55 us -> 1.52 us  [share(): return lax.dynamic_slice_in_dim(array, narrow_pos * length, length, 0)]
  transfers between devices with their start and end apart: 3 -> 0, of which waited for: 2 -> 0; matrix products, arithmetic and copies ran while one was open for 5% -> 0% of each run, Pallas kernels for 0% -> 0%
where the time goes in v1:
time: 138 us
  Pallas kernels  127 us (92%)
  local copies, waits for them, and re-layouts  8.1 us (6%)
  other arithmetic  2.87 us (2%)
    pallas_call x1, Pallas kernels, scatter_all(): pl.pallas_call(functools.partial(scatter_kernel, *counts, score_scale), o...  79.2 us
    pallas_call x1, Pallas kernels, gather_all(): pl.pallas_call(functools.partial(gather_kernel, *counts), out_shape=(jax....  26.6 us
    pallas_call x1, Pallas kernels, work(): pl.pallas_call(functools.partial(work_kernel, score_scale), out_shape=(ja...  20.7 us

profile of v1, /device:TPU:0, one launch (start us, length us, event | category | flops | bytes accessed | tf_op | source)
XLA Modules:
  0.0 138.2 jit_solution(11742199474140899735)
XLA Ops:
  0.6 0.7 convert_bitcast_fusion
  1.3 0.7 convert_element_type.45
  2.0 0.8 dynamic_slice.12
  2.7 0.8 dynamic_slice.13
  3.5 0.8 dynamic-slice_convert_fusion
  4.2 0.8 reshape.45
  5.0 0.1 dynamic-slice_convert_fusion.1
  5.1 0.1 concatenate.3
  5.2 0.6 pad_bitcast_fusion.aux_ref
  5.8 26.6 %shard_map.95 = (bf16[32,256,128]{2,1,0:T(8,128)(2,1)}, f32[32,8,128]{2,1,0:T(8,128)}) custom-call(bf16[256,128]{1,0:T(8,128)(2,1)} %query_ref.1, f32[8,128]{1,0:T(8,128)} %pad_bitcast_fusion.aux_ref), custom_call_target="tpu_custom_call" | custom-call | tf_op jit(solution)/shard_map/pallas_call | solution.py:119
  32.4 0.9 copy.12
  33.3 0.7 convert_element_type.53.negs_ref
  34.0 0.1 slice_convert_fusion.2
  34.1 0.6 convert_element_type.51.pos_ref
  34.7 0.7 convert_element_type.49.local_ref
  35.4 0.7 convert_element_type.47.owner_ref
  36.0 0.0 copy-start
  36.1 0.6 subtract_multiply_fusion.bias_ref
  36.7 0.0 copy-done
  36.7 20.7 %shard_map.96 = (f32[64,128,128]{2,1,0:T(8,128)}, f32[8192,128]{1,0:T(8,128)}) custom-call(s32[1]{0:T(128)} %bitcast.me_ref, s32[512]{0:T(512)} %convert_element_type.47.owner_ref, s32[512]{0:T(512)} %convert_element_type.49.local_ref, bf16[8192,128]{1,0:T(8,128)(2,1)} %index_ref.1, bf16[8192,128]{1,0:T(8,128)(2,1)} %bitcast.12, ...), custom_call_target="tpu_custom_call" | custom-call | tf_op jit(solution)/shard_map/pallas_call | solution.py:221
  57.4 79.2 %shard_map.97 = f32[256,128]{1,0:T(8,128)} custom-call(f32[32,2,128,128]{3,2,1,0:T(8,128)} %bitcast.11), custom_call_target="tpu_custom_call" | custom-call | tf_op jit(solution)/shard_map/pallas_call | solution.py:343
  136.6 1.6 %copy.14 = f32[256,128]{1,0:T(8,128)} copy(f32[256,128]{1,0:T(8,128)} %shard_map.97) | data formatting | bytes 262144
  (4 shorter events, 0.0 us)
Async XLA Ops:
  36.0 0.6 copy-start

commit v2 on v1

v2 whole, which is shorter than its diff:
```python
import functools
import math

import jax
import jax.numpy as jnp
from jax import lax
from jax.experimental import pallas as pl
from jax.experimental.pallas import tpu as pltpu
from jax.sharding import PartitionSpec as P

BLOCK = 128
QTILE = 128
CAP = 2
LANES = 128
CORES = 2
MESH = pl.DeviceIdType.MESH
VMEM_LIMIT = 56 * 1024 * 1024
FAR_BELOW = -1e30


def place_counts(wide_count, narrow_count):
    x_count = 1 << (int(math.log2(narrow_count)) // 2)
    return wide_count // CORES, narrow_count // x_count, x_count


def coordinates(x_count):
    wide, narrow = lax.axis_index("wide"), lax.axis_index("narrow")
    return wide // CORES, wide % CORES, narrow // x_count, narrow % x_count


def greet(peers):
    barrier = pltpu.get_barrier_semaphore()
    for peer in peers:
        pl.semaphore_signal(barrier, inc=1, device_id=peer, device_id_type=MESH)
    pl.semaphore_wait(barrier, len(peers))


def gather_kernel(
    y_count,
    z_count,
    x_count,
    query_ref,
    aux_ref,
    index_ref,
    query_all,
    aux_all,
    index_other,
    own_sem,
    index_sem,
    *sems,
):
    y, core, z, x = coordinates(x_count)
    narrow_count = z_count * x_count

    def device(dy, dz, dx):
        wide = lax.rem(y + dy, y_count) * CORES + core
        return wide, lax.rem(z + dz, z_count) * x_count + lax.rem(x + dx, x_count)

    def number(place):
        return place[0] // CORES * narrow_count + place[1]

    plane = [(dy, dx) for dy in range(y_count) for dx in range(x_count)][1:]
    z_peers = [device(0, dz, 0) for dz in range(1, z_count)]
    plane_peers = [device(dy, 0, dx) for dy, dx in plane]
    buddy = (y * CORES + 1 - core, z * x_count + x)
    greet(z_peers + plane_peers + [buddy])
    me = number(device(0, 0, 0))
    pairs = (
        (query_ref, query_all, sems[0], sems[1]),
        (aux_ref, aux_all, sems[2], sems[3]),
    )
    sent = []

    def send(chunk, peer, own):
        for source, whole, send_sem, recv_sem in pairs:
            copy = pltpu.make_async_remote_copy(
                src_ref=source if own else whole.at[chunk],
                dst_ref=whole.at[chunk],
                send_sem=send_sem.at[len(sent) // 2],
                recv_sem=recv_sem.at[chunk],
                device_id=peer,
                device_id_type=MESH,
            )
            copy.start()
            sent.append(copy)

    def arrive(chunk):
        for source, whole, send_sem, recv_sem in pairs:
            pltpu.make_async_remote_copy(
                src_ref=source,
                dst_ref=whole.at[chunk],
                send_sem=send_sem.at[0],
                recv_sem=recv_sem.at[chunk],
                device_id=buddy,
                device_id_type=MESH,
            ).wait_recv()

    for peer in z_peers + plane_peers:
        send(me, peer, True)
    to_buddy = pltpu.make_async_remote_copy(
        src_ref=index_ref,
        dst_ref=index_other,
        send_sem=index_sem.at[0],
        recv_sem=index_sem.at[1],
        device_id=buddy,
        device_id_type=MESH,
    )
    to_buddy.start()
    local = [
        pltpu.make_async_copy(source, whole.at[me], own_sem.at[i])
        for i, (source, whole, _, _) in enumerate(pairs)
    ]
    for copy in local:
        copy.start()
    for dz in range(1, z_count):
        chunk = number(device(0, dz, 0))
        arrive(chunk)
        for peer in plane_peers:
            send(chunk, peer, False)
    for dz in range(z_count):
        for dy, dx in plane:
            arrive(number(device(dy, dz, dx)))
    for copy in sent:
        copy.wait_send()
    for copy in local:
        copy.wait()
    to_buddy.wait()


def gather_all(queries, aux, index_rows, counts):
    y_count, z_count, x_count = counts
    devices = y_count * z_count * x_count
    sends = (z_count - 1) + (y_count * x_count - 1) * z_count
    vmem, anywhere = (pl.BlockSpec(memory_space=m) for m in (pltpu.VMEM, pl.ANY))
    return pl.pallas_call(
        functools.partial(gather_kernel, *counts),
        out_shape=(
            jax.ShapeDtypeStruct((devices, *queries.shape), queries.dtype),
            jax.ShapeDtypeStruct((devices, *aux.shape), aux.dtype),
            jax.ShapeDtypeStruct(index_rows.shape, index_rows.dtype),
        ),
        in_specs=[vmem, vmem, anywhere],
        out_specs=[vmem, vmem, anywhere],
        scratch_shapes=[
            pltpu.SemaphoreType.DMA((2,)),
            pltpu.SemaphoreType.DMA((2,)),
            pltpu.SemaphoreType.DMA((sends,)),
            pltpu.SemaphoreType.DMA((devices,)),
            pltpu.SemaphoreType.DMA((sends,)),
            pltpu.SemaphoreType.DMA((devices,)),
        ],
        compiler_params=pltpu.CompilerParams(
            collective_id=0, has_side_effects=True, vmem_limit_bytes=VMEM_LIMIT
        ),
    )(queries, aux, index_rows)


def work_kernel(
    score_scale,
    groups,
    place_ref,
    owner_ref,
    local_ref,
    index_ref,
    other_ref,
    query_ref,
    bias_ref,
    loss_ref,
    pos_ref,
    negs_ref,
    dq_ref,
    index_grad_ref,
    other_grad_ref,
    slots,
    places,
    index_both,
    grads,
    bias_now,
    rel_now,
    block_sum,
    sems,
):
    group_tiles = bias_ref.shape[0] // groups
    group_slots = owner_ref.shape[0] // groups
    row_count = index_ref.shape[0]
    chunk_tiles = min(4, group_tiles)
    chunk = chunk_tiles * QTILE
    mine, other = place_ref[0], place_ref[1]
    log2_scale = score_scale * math.log2(math.e)
    loads = [
        pltpu.make_async_copy(source, index_both.at[pl.ds(i * row_count, row_count), :], sems.at[i])
        for i, source in enumerate((index_ref, other_ref))
    ]
    for load in loads:
        load.start()
    dq_ref[...] = jnp.zeros_like(dq_ref)
    grads[...] = jnp.zeros_like(grads)
    row_ids = lax.broadcasted_iota(jnp.int32, (BLOCK, QTILE), 0)

    def list_group(group):
        def list_one(slot, count):
            owner = owner_ref[group * group_slots + slot]
            place = local_ref[group * group_slots + slot] * BLOCK
            slots[group, count] = slot
            places[group, count] = place + jnp.where(owner == other, row_count, 0)
            return count + jnp.logical_or(owner == mine, owner == other).astype(jnp.int32)

        count = lax.fori_loop(0, group_slots, list_one, jnp.int32(0), unroll=8)
        slots[group, count] = -1
        places[group, count] = 0
        return count

    counts = [list_group(group) for group in range(groups)]
    for load in loads:
        load.wait()
    for group in range(groups):
        tiles = pl.ds(group * group_tiles, group_tiles)

        @pl.loop(0, (counts[group] + 1) // 2)
        def _(pair):
            rows, blocks, blocks_t = [], [], []
            for h in range(2):
                slot = slots[group, 2 * pair + h]
                place = pl.multiple_of(places[group, 2 * pair + h], BLOCK)
                rows.append(pl.ds(place, BLOCK))
                blocks.append(index_both[rows[h], :])
                blocks_t.append(blocks[h].astype(jnp.float32).T.astype(jnp.bfloat16))
                hit = jnp.any(negs_ref[tiles, :] == slot, axis=1, keepdims=True)
                rel = pos_ref[tiles, :] - slot * BLOCK
                inside = jnp.logical_and(rel >= 0, rel < BLOCK)
                bias_now[h] = jnp.where(
                    jnp.logical_or(hit, inside), bias_ref[tiles, :], FAR_BELOW
                )
                rel_now[h] = rel
            block = jnp.concatenate(blocks, axis=0)
            block_t = jnp.concatenate(blocks_t, axis=1)
            for turn in range(group_tiles // chunk_tiles):
                first = group * group_tiles + turn * chunk_tiles
                query = query_ref[pl.ds(first * QTILE, chunk), :]
                scores = lax.dot_general(
                    block, query, (((1,), (1,)), ((), ())), preferred_element_type=jnp.float32
                )
                halves = []
                for h in range(2):
                    parts = []
                    for t in range(chunk_tiles):
                        at = turn * chunk_tiles + t
                        part = scores[h * BLOCK : (h + 1) * BLOCK, t * QTILE : (t + 1) * QTILE]
                        grown = jnp.exp2(part * log2_scale + bias_now[h, at : at + 1, :])
                        less = grown - loss_ref[first + t : first + t + 1, :]
                        grad = jnp.where(row_ids == rel_now[h, at : at + 1, :], less, grown)
                        parts.append(grad.astype(jnp.bfloat16))
                    halves.append(jnp.concatenate(parts, axis=1))
                logit_grad = jnp.concatenate(halves, axis=0)
                added = jnp.dot(logit_grad, query, preferred_element_type=jnp.float32)
                if turn == 0:
                    block_sum[...] = added
                else:
                    block_sum[...] += added
                part = jnp.dot(block_t, logit_grad, preferred_element_type=jnp.float32)
                for t in range(chunk_tiles):
                    dq_ref[first + t] += part[:, t * QTILE : (t + 1) * QTILE]
            for h in range(2):
                total = block_sum[h * BLOCK : (h + 1) * BLOCK, :] * score_scale
                grads[rows[h], :] += total.astype(jnp.bfloat16).astype(jnp.float32)

    store = pltpu.make_async_copy(grads.at[pl.ds(0, row_count), :], index_grad_ref, sems.at[2])
    store.start()
    other_grad_ref[...] = grads[row_count:, :].astype(jnp.bfloat16)
    store.wait()


def work(place, owner, local, index_rows, index_other, query_all, small, score_scale):
    row_count, feat_width = index_rows.shape
    tile_total = small[0].shape[0]
    groups = lax.axis_size("wide") // CORES
    group_tiles = tile_total // groups
    smem, vmem, anywhere = (
        pl.BlockSpec(memory_space=m) for m in (pltpu.SMEM, pltpu.VMEM, pl.ANY)
    )
    names = (groups, owner.shape[0] // groups + 1)
    return pl.pallas_call(
        functools.partial(work_kernel, score_scale, groups),
        out_shape=(
            jax.ShapeDtypeStruct((tile_total, feat_width, QTILE), jnp.float32),
            jax.ShapeDtypeStruct(index_rows.shape, jnp.float32),
            jax.ShapeDtypeStruct(index_rows.shape, jnp.bfloat16),
        ),
        in_specs=[smem] * 3 + [anywhere] * 2 + [vmem] * 5,
        out_specs=[vmem, anywhere, vmem],
        scratch_shapes=[
            pltpu.SMEM(names, jnp.int32),
            pltpu.SMEM(names, jnp.int32),
            pltpu.VMEM((2 * row_count, feat_width), jnp.bfloat16),
            pltpu.VMEM((2 * row_count, feat_width), jnp.float32),
            pltpu.VMEM((2, group_tiles, QTILE), jnp.float32),
            pltpu.VMEM((2, group_tiles, QTILE), jnp.int32),
            pltpu.VMEM((2 * BLOCK, feat_width), jnp.float32),
            pltpu.SemaphoreType.DMA((3,)),
        ],
        compiler_params=pltpu.CompilerParams(vmem_limit_bytes=VMEM_LIMIT),
    )(place, owner, local, index_rows, index_other, query_all, *small)


def scatter_kernel(
    y_count,
    z_count,
    x_count,
    score_scale,
    part_ref,
    grad_ref,
    out_ref,
    grad_other,
    plane_send,
    plane_recv,
    column_send,
    column_recv,
    a_sem,
    *sems,
):
    y, core, z, x = coordinates(x_count)
    narrow_count = z_count * x_count
    b_send, b_recv, c_send, c_recv = sems

    def device(dy, dz, dx):
        wide = lax.rem(y + dy, y_count) * CORES + core
        return wide, lax.rem(z + dz, z_count) * x_count + lax.rem(x + dx, x_count)

    def number(place):
        return place[0] // CORES * narrow_count + place[1]

    def remote(source, target, send_sem, recv_sem, peer):
        return pltpu.make_async_remote_copy(
            src_ref=source,
            dst_ref=target,
            send_sem=send_sem,
            recv_sem=recv_sem,
            device_id=peer,
            device_id_type=MESH,
        )

    shifts = [(dy, dx) for dy in range(y_count) for dx in range(x_count)]
    buddy = (y * CORES + 1 - core, z * x_count + x)
    z_peers = [device(0, dz, 0) for dz in range(1, z_count)]
    plane_peers = [device(dy, 0, dx) for dy, dx in shifts[1:]]
    greet(z_peers + plane_peers + [buddy])
    z_order = list(range(1, z_count)) + [0]
    to_buddy = remote(grad_ref, grad_other, a_sem.at[0], a_sem.at[1], buddy)
    to_buddy.start()
    in_plane, columns = {}, {}
    for dz in z_order:
        for p in range(1, len(shifts)):
            slot = (p - 1) * z_count + dz
            dy, dx = shifts[p]
            plane_send[slot] = part_ref[number(device(dy, dz, dx))].astype(jnp.bfloat16)
            in_plane[p, dz] = remote(
                plane_send.at[slot],
                plane_recv.at[slot],
                b_send.at[slot],
                b_recv.at[slot],
                plane_peers[p - 1],
            )
            in_plane[p, dz].start()
    for dz in z_order:
        total = part_ref[number(device(0, dz, 0))]
        for p in range(1, len(shifts)):
            in_plane[p, dz].wait_recv()
            total += plane_recv[(p - 1) * z_count + dz].astype(jnp.float32)
        if dz:
            column_send[dz - 1] = total.astype(jnp.bfloat16)
            columns[dz] = remote(
                column_send.at[dz - 1],
                column_recv.at[dz - 1],
                c_send.at[dz - 1],
                c_recv.at[dz - 1],
                z_peers[dz - 1],
            )
            columns[dz].start()
    for dz in range(1, z_count):
        columns[dz].wait_recv()
        total += column_recv[dz - 1].astype(jnp.float32)
    for t in range(total.shape[0]):
        out_ref[t * QTILE : (t + 1) * QTILE, :] = total[t].T * score_scale
    for copy in [*in_plane.values(), *columns.values()]:
        copy.wait_send()
    to_buddy.wait()


def scatter_all(partial, other_grad, counts, score_scale):
    y_count, z_count, x_count = counts
    devices, tiles, feat_width, width = partial.shape
    passed = devices - z_count
    block = (tiles, feat_width, width)
    vmem, anywhere = (pl.BlockSpec(memory_space=m) for m in (pltpu.VMEM, pl.ANY))
    return pl.pallas_call(
        functools.partial(scatter_kernel, *counts, score_scale),
        out_shape=(
            jax.ShapeDtypeStruct((tiles * width, feat_width), jnp.float32),
            jax.ShapeDtypeStruct(other_grad.shape, other_grad.dtype),
        ),
        in_specs=[vmem, anywhere],
        out_specs=[vmem, anywhere],
        scratch_shapes=[
            pltpu.VMEM((passed, *block), jnp.bfloat16),
            pltpu.VMEM((passed, *block), jnp.bfloat16),
            pltpu.VMEM((z_count - 1, *block), jnp.bfloat16),
            pltpu.VMEM((z_count - 1, *block), jnp.bfloat16),
            pltpu.SemaphoreType.DMA((2,)),
            pltpu.SemaphoreType.DMA((passed,)),
            pltpu.SemaphoreType.DMA((passed,)),
            pltpu.SemaphoreType.DMA((z_count - 1,)),
            pltpu.SemaphoreType.DMA((z_count - 1,)),
        ],
        compiler_params=pltpu.CompilerParams(
            collective_id=1, has_side_effects=True, vmem_limit_bytes=VMEM_LIMIT
        ),
    )(partial, other_grad)


def shards(
    queries, index_rows, lse_shift, loss_weight, positives, tile_negs, fetch_owner, fetch_local
):
    wide_count = lax.axis_size("wide")
    narrow_count = lax.axis_size("narrow")
    devices = wide_count // CORES * narrow_count
    counts = place_counts(wide_count, narrow_count)
    narrow_pos = lax.axis_index("narrow")
    feat_width = queries.shape[1]
    own_queries = queries.shape[0]
    fetch_count = fetch_local.shape[0]
    negs_width = tile_negs.shape[1]
    score_scale = 2.0 / math.sqrt(feat_width)

    def share(array):
        length = array.shape[0] // narrow_count
        return lax.dynamic_slice_in_dim(array, narrow_pos * length, length, 0)

    pieces = [
        share(lse_shift),
        share(loss_weight),
        share(positives).astype(jnp.float32),
        share(tile_negs.reshape(-1)).astype(jnp.float32),
        fetch_owner[:, 0].astype(jnp.float32),
        fetch_local.astype(jnp.float32),
    ]
    lengths = [p.shape[0] for p in pieces]
    used = sum(lengths)
    padded = -(-used // (8 * LANES)) * 8 * LANES
    aux = jnp.pad(jnp.concatenate(pieces), (0, padded - used)).reshape(-1, LANES)
    query_all, aux_all, index_other = gather_all(queries, aux, index_rows, counts)
    aux_all = aux_all.reshape(devices, padded)
    unpacked, start = [], 0
    for length in lengths:
        unpacked.append(aux_all[:, start : start + length].reshape(-1))
        start += length
    lse, loss, pos, negs, owner, local = unpacked
    lse_full = lse + math.log(fetch_count * narrow_count * BLOCK)
    bias = ((jnp.log(loss) - lse_full) * math.log2(math.e)).reshape(-1, QTILE)
    wide_pos = lax.axis_index("wide")
    buddy_pos = wide_pos + 1 - 2 * (wide_pos % CORES)
    place = jnp.stack([wide_pos * narrow_count + narrow_pos, buddy_pos * narrow_count + narrow_pos])
    small = (
        bias,
        loss.reshape(-1, QTILE),
        pos.astype(jnp.int32).reshape(-1, QTILE),
        negs.astype(jnp.int32).reshape(-1, negs_width),
    )
    partial, index_grad, other_grad = work(
        place,
        owner.astype(jnp.int32),
        local.astype(jnp.int32),
        index_rows,
        index_other,
        query_all.reshape(-1, feat_width),
        small,
        score_scale,
    )
    tiles = own_queries // QTILE
    query_grad, more_grad = scatter_all(
        partial.reshape(devices, tiles, feat_width, QTILE), other_grad, counts, score_scale
    )
    return query_grad, index_grad + more_grad.astype(jnp.float32)


def solution(mesh):
    in_specs = (
        P(("wide", "narrow"), None),
        P(("wide", "narrow"), None),
        P("wide"),
        P("wide"),
        P("wide"),
        P("wide", None),
        P(("wide", "narrow"), None),
        P(("wide", "narrow")),
    )
    out_specs = (P(("wide", "narrow"), None), P(("wide", "narrow"), None))
    return jax.shard_map(shards, mesh=mesh, in_specs=in_specs, out_specs=out_specs, check_vma=False)
```

time: 138 us -> 91.4 us (0.66)
  Pallas kernels: 127 us -> 76.7 us
  other arithmetic: 2.87 us -> 7.48 us
    pallas_call x1, Pallas kernels: 79.2 us -> 18.8 us  [scatter_all(): pl.pallas_call(functools.partial(scatter_kernel, *counts, score_scale), o...]
    pallas_call x1, Pallas kernels: 20.7 us -> 33.1 us  [work(): pl.pallas_call(functools.partial(work_kernel, score_scale, groups), out_s...]
    add x0 -> x1, other arithmetic: none -> 3.98 us  [shards(): return (query_grad, index_grad + more_grad.astype(jnp.float32))]
    pallas_call x1, Pallas kernels: 26.6 us -> 24.8 us  [gather_all(): pl.pallas_call(functools.partial(gather_kernel, *counts), out_shape=(jax....]
where the time goes in v2:
time: 91.4 us; the launch traced here: 92 us
  Pallas kernels  76.7 us (84%)
  other arithmetic  7.48 us (8%)
  local copies, waits for them, and re-layouts  7.05 us (8%)
    pallas_call x1, Pallas kernels, work(): pl.pallas_call(functools.partial(work_kernel, score_scale, groups), out_s...  33.1 us
    pallas_call x1, Pallas kernels, gather_all(): pl.pallas_call(functools.partial(gather_kernel, *counts), out_shape=(jax....  24.8 us
    pallas_call x1, Pallas kernels, scatter_all(): pl.pallas_call(functools.partial(scatter_kernel, *counts, score_scale), o...  18.8 us
    add x1, other arithmetic, shards(): return (query_grad, index_grad + more_grad.astype(jnp.float32))  3.98 us

profile of v2, /device:TPU:0, one launch (start us, length us, event | category | flops | bytes accessed | tf_op | source)
XLA Modules:
  0.0 92.0 jit_solution(11389521633978379063)
XLA Ops:
  0.6 0.6 pad_add_fusion.place_ref
  1.3 0.7 convert_bitcast_fusion
  2.0 0.7 convert_element_type.48
  2.6 0.8 dynamic_slice.12
  3.4 0.8 dynamic_slice.13
  4.1 0.8 dynamic-slice_convert_fusion
  4.9 0.8 reshape.41
  5.7 0.1 dynamic-slice_convert_fusion.1
  5.7 0.1 concatenate.3
  5.8 0.6 pad_bitcast_fusion.aux_ref
  6.4 24.8 %shard_map.95 = (bf16[16,256,128]{2,1,0:T(8,128)(2,1)}, f32[16,8,128]{2,1,0:T(8,128)}, bf16[8192,128]{1,0:T(8,128)(2,1)}) custom-call(bf16[256,128]{1,0:T(8,128)(2,1)} %query_ref.1, f32[8,128]{1,0:T(8,128)} %pad_bitcast_fusion.aux_ref, bf16[8192,128]{1,0:T(8,128)(2,1)} %index_ref.3), custom_call_target="tpu_custom_call" | custom-call | tf_op jit(solution)/shard_map/pallas_call | solution.py:135
  31.2 0.9 copy.12
  32.1 0.7 convert_element_type.56.negs_ref
  32.7 0.1 slice_convert_fusion.2
  32.8 0.6 convert_element_type.54.pos_ref
  33.4 0.7 convert_element_type.52.local_ref
  34.1 0.6 convert_element_type.50.owner_ref
  34.7 0.6 subtract_multiply_fusion.bias_ref
  35.3 33.1 %shard_map.96 = (f32[32,128,128]{2,1,0:T(8,128)}, f32[8192,128]{1,0:T(8,128)}, bf16[8192,128]{1,0:T(8,128)(2,1)}) custom-call(s32[2]{0:T(128)} %pad_add_fusion.place_ref, s32[256]{0:T(256)} %convert_element_type.50.owner_ref, s32[256]{0:T(256)} %convert_element_type.52.local_ref, bf16[8192,128]{1,0:T(8,128)(2,1)} %index_ref.3, ...), custom_call_target="tpu_custom_call" | custom-call | tf_op jit(solution)/shard_map/pallas_call | solution.py:282
  68.5 0.0 copy-start
  68.5 18.8 %shard_map.97 = (f32[256,128]{1,0:T(8,128)}, bf16[8192,128]{1,0:T(8,128)(2,1)}) custom-call(f32[16,2,128,128]{3,2,1,0:T(8,128)} %bitcast.12, bf16[8192,128]{1,0:T(8,128)(2,1)} %get-tuple-element.14.grad_ref), custom_call_target="tpu_custom_call" | custom-call | tf_op jit(solution)/shard_map/pallas_call | solution.py:395
  87.3 0.0 copy-done
  87.4 4.0 %convert_add_fusion = f32[8192,128]{1,0:T(8,128)} fusion(f32[8192,128]{1,0:T(8,128)S(1)} %copy-done, bf16[8192,128]{1,0:T(8,128)(2,1)} %get-tuple-element.17), kind=kLoop, calls=%fused_computation | loop fusion | flops 2097152 | bytes 10485760 | tf_op jit(solution)/shard_map/add | solution.py:482
  91.3 0.7 copy.14
  (8 shorter events, 0.0 us)
Async XLA Ops:
  34.7 0.6 copy-start.1
  68.5 18.9 %copy-start = (f32[8192,128]{1,0:T(8,128)S(1)}, f32[8192,128]{1,0:T(8,128)}, u32[]{:S(2)}) copy-start(f32[8192,128]{1,0:T(8,128)} %get-tuple-element.16) | copy-start | bytes 12582916
  87.3 4.0 %copy-start.2 = (f32[256,128]{1,0:T(8,128)S(1)}, f32[256,128]{1,0:T(8,128)}, u32[]{:S(2)}) copy-start(f32[256,128]{1,0:T(8,128)} %get-tuple-element.25) | copy-start | bytes 393220
